TPU v7x, 512 devices: a whole 4x4x16 slice. The times are simulated.
512 devices in a mesh: dp: 4 (over x), expert: 16 (over z_hi, y, core), tensor: 8 (over z_lo).
Axes of the slice: x: 4, y: 4, z: 16 (z_hi: 2, z_lo: 8; z = z_hi * 8 + z_lo), core: 2. Of those that a mesh axis runs over, the one named last changes fastest.
Arguments:
- layer_grad: bfloat16 [8192, 4096], P(('dp', 'expert'), 'tensor'), may hold values from -6 to 6
- gate_probs: float32 [8192, 2], P(('dp', 'expert')), may hold values from 0.2 to 1
- expert_ids: int32 [8192, 2], P(('dp', 'expert')), may hold values from 0 to 15, all different within a row; in each aligned block of 128 rows (0 to 127, 128 to 255, ...) at most 20 rows name the same one
- down_weight: bfloat16 [16, 12288, 4096], P('expert', ('dp', 'tensor')), may hold values from -0.09375 to 0.09375
Outputs:
- hidden_grad: bfloat16 [16, 1280, 12288], P('expert', None, ('dp', 'tensor'))
Inputs may be any that keep to these rules, and one draw needn't show every extreme that they name: `expert_ids`: within the rows of one token group (128 aligned rows) the two experts of a row differ, no expert is named more than 20 times, a bound that some block reaches.
All inputs are finite; a program needn't handle non-finite values.
Results may differ from a plain program's by a relative error of at most 0.0049.
Values may be sent and summed in bfloat16 or wider, within the bound.
A program may use at most 64 MiB of HBM per device.

v0:
```python
import jax
import jax.numpy as jnp
from jax import lax
from jax.sharding import PartitionSpec as P


def route_rows(features, gate_probs, expert_ids, experts, capacity):
    tokens = features.shape[0]
    flat = expert_ids.reshape(-1)
    onehot = (flat[:, None] == jnp.arange(experts, dtype=jnp.int32)[None, :]).astype(jnp.int32)
    ranks = jnp.sum((jnp.cumsum(onehot, axis=0) - onehot) * onehot, axis=1)
    places = (flat * capacity + ranks).reshape(tokens, 2)
    slot_rows = jnp.arange(experts * capacity, dtype=jnp.int32)[:, None]
    mixing = jnp.zeros((experts * capacity, tokens), jnp.float32)
    for choice_k in range(2):
        mixing = mixing + jnp.where(
            slot_rows == places[None, :, choice_k], gate_probs[None, :, choice_k], 0.0
        )
    routed = jnp.dot(
        mixing,
        features.astype(jnp.float32),
        precision=lax.Precision.HIGHEST,
        preferred_element_type=jnp.float32,
    )
    return routed.astype(jnp.bfloat16).reshape(experts, 1, capacity, features.shape[1])


def body(layer_grad, gate_probs, expert_ids, down_weight):
    local_experts = down_weight.shape[0]
    experts = local_experts * lax.axis_size("expert")
    capacity = layer_grad.shape[0] * 2 * 5 // (4 * experts)
    routed = route_rows(layer_grad, gate_probs, expert_ids, experts, capacity)
    arrived = lax.all_to_all(routed, "expert", split_axis=0, concat_axis=1, tiled=True)
    full_rows = lax.all_gather(arrived, "tensor", axis=3, tiled=True)
    hidden = jnp.einsum(
        "xscd,xhd->xsch",
        lax.all_gather(full_rows, "dp", axis=1, tiled=True),
        down_weight,
        preferred_element_type=jnp.float32,
    ).astype(jnp.bfloat16)
    return hidden.reshape(local_experts, -1, down_weight.shape[1])


def solution(mesh):
    placed = (
        P(("dp", "expert"), "tensor"),
        P(("dp", "expert"), None),
        P(("dp", "expert"), None),
        P("expert", ("dp", "tensor"), None),
    )
    return jax.shard_map(
        body,
        mesh=mesh,
        in_specs=placed,
        out_specs=P("expert", None, ("dp", "tensor")),
        check_vma=False,
    )
```

profile of v0, /device:TPU:1, one launch (start us, length us, event | category | flops | bytes accessed | tf_op | source)
XLA Modules:
  0.0 256.0 jit_solution(12049527696230808316)
XLA Ops:
  6.5 0.0 copy-start
  6.5 0.0 all-gather.5.cloned.1.call-start
  6.5 0.9 copy.28
  7.5 0.1 eq.60
  7.6 0.1 eq.56
  7.8 0.8 slice_bitcast_fusion.2
  8.5 0.6 reduce-window.6
  9.1 0.2 slice_reduce_fusion
  9.3 0.1 fusion.18
  9.4 0.1 reduce_sum.12
  9.6 0.1 copy.31
  9.6 0.7 multiply_add_fusion
  10.4 2.0 convolution_convert_fusion
  12.4 1.0 reshape.43
  13.4 37.0 %all_to_all.12 = bf16[16,1,20,512]{3,2,1,0:T(8,128)(2,1)S(1)} all-to-all(bf16[16,1,20,512]{3,2,1,0:T(8,128)(2,1)S(1)} %bitcast.40), channel_id=1, replica_groups=mesh['dp'=4,'expert'=16,'tensor'=8] {'expert'}, dimensions={0} | all-to-all | bytes 655360 | tf_op jit(solution)/shard_map/all_to_all | solution.py:33
  50.4 0.8 copy.33
  51.2 0.0 all-gather.5.cloned.1.call-update
  51.3 0.0 all-gather.7.cloned.1.call-start
  51.3 78.4 %all-gather.5.cloned.1.call-done = bf16[16,1,20,4096]{3,0,2,1:T(8,128)(2,1)} async-done(((bf16[16,1,20,512]{3,0,2,1:T(8,128)(2,1)}), bf16[16,1,20,4096]{3,0,2,1:T(8,128)(2,1)}) %all-gather.5.cloned.1.call-update) | async-done | bytes 2621456 | tf_op jit(solution)/shard_map/all_gather | solution.py:34
  129.7 0.0 all-gather.7.cloned.1.call-update
  129.8 107.2 %all-gather.7.cloned.1.call-done = bf16[64,1,20,4096]{3,0,2,1:T(8,128)(2,1)} async-done(((bf16[16,1,20,4096]{3,0,2,1:T(8,128)(2,1)}), bf16[64,1,20,4096]{3,0,2,1:T(8,128)(2,1)}) %all-gather.7.cloned.1.call-update) | async-done | bytes 10485776 | tf_op jit(solution)/shard_map/all_gather | solution.py:37
  237.0 0.0 copy-done
  237.0 8.4 %fusion.3 = bf16[64,20,384]{2,0,1:T(8,128)(2,1)S(1)} fusion(bf16[1,384,4096]{2,1,0:T(8,128)(2,1)S(1)} %copy-done, bf16[64,1,20,4096]{3,0,2,1:T(8,128)(2,1)} %all-gather.7.cloned.1.call-done), kind=kOutput, calls=%fused_computation.3 | convolution fusion | flops 4027023360 | bytes 14614528 | tf_op jit(solution)/shard_map/xscd,xhd->xsch/dot_general | solution.py:35
  245.4 1.6 copy.34
  247.0 2.1 reshape.46
  (4 shorter events, 0.1 us)
Async XLA Ops:
  6.5 230.4 %copy-start = (bf16[1,384,4096]{2,1,0:T(8,128)(2,1)S(1)}, bf16[1,384,4096]{2,1,0:T(8,128)(2,1)}, u32[]{:S(2)}) copy-start(bf16[1,384,4096]{2,1,0:T(8,128)(2,1)} %param.7) | copy-start | bytes 9437188
  6.5 123.2 %all-gather.5.cloned.1.call-start = ((), (), s32[]{:S(2)}) async-start(), calls=%async_computation.1 | async-start | bytes 2949120 | tf_op jit(solution)/shard_map/all_gather | solution.py:34
  51.3 185.7 %all-gather.7.cloned.1.call-start = ((), (), s32[]{:S(2)}) async-start(), calls=%async_computation.2 | async-start | bytes 13107200 | tf_op jit(solution)/shard_map/all_gather | solution.py:37
Sparse Core Ops, SparseCore 0:
  51.4 78.3 all-gather.4
  131.8 105.0 all-gather.6
where the time goes:
time: 256 us
  waiting for transfers between devices  186 us (73%)
  blocking collectives  37 us (14%)
  between operations  13.4 us (5%)
  matrix products  10.5 us (4%)
  local copies, waits for them, and re-layouts  7.95 us (3%)
    all_gather x1, waiting for transfers between devices, body(): lax.all_gather(full_rows, 'dp', axis=1, tiled=True)  107 us
    all_gather x1, waiting for transfers between devices, body(): full_rows = lax.all_gather(arrived, 'tensor', axis=3, tiled=True)  78.4 us
    all_to_all x1, blocking collectives, body(): lax.all_to_all(routed, 'expert', split_axis=0, concat_axis=1, tiled=True)  37 us
    dot_general x1, matrix products, body(): jnp.einsum('xscd,xhd->xsch', lax.all_gather(full_rows, 'dp', axis=1, tile...  8.42 us
  transfers between devices with their start and end apart: 2, of which 2 were waited for; matrix products, arithmetic and copies ran while one was open for 0% of the time, Pallas kernels for 0%

commit v1 on v0

v1 whole, which is shorter than its diff:
```python
import functools

import jax
import jax.numpy as jnp
from jax import lax
from jax.experimental import pallas as pl
from jax.experimental.pallas import tpu as pltpu
from jax.sharding import PartitionSpec as P

MESH = pl.DeviceIdType.MESH
MAIN = 16
TAIL = 4


def kernel(
    shape,
    feats, probs, ids, weight, out,
    routed, rows, passing, held_w, acc, acc_tail, w_sem,
    a_send, a_recv, z_send, z_recv, t_send, t_recv, x_send, x_recv, f_send, f_recv,
):
    dp, yc, zl, width = shape
    half = zl // 2
    ring = 2 * zl
    quarter = width // 4
    experts = 2 * yc
    x = lax.axis_index("dp")
    ex = lax.axis_index("expert")
    j = lax.axis_index("tensor")
    zh, c = ex // yc, ex % yc
    p = zh * zl + j

    def at_ring(pos):
        pos = (pos + ring) % ring
        return {"expert": (pos // zl) * yc + c, "tensor": pos % zl}

    def at_x(offset):
        return {"dp": (x + offset + dp) % dp}

    def at_c(offset):
        return {"expert": zh * yc + (c + offset) % yc}

    barrier = pltpu.get_barrier_semaphore()
    partners = [at_ring(p + 1), at_ring(p - 1), at_x(1), at_x(-1)] + [at_c(i) for i in range(1, yc)]
    for partner in partners:
        pl.semaphore_signal(barrier, inc=1, device_id=partner, device_id_type=MESH)

    w_copy = pltpu.make_async_copy(weight.at[0], held_w, w_sem)
    w_copy.start()

    tokens = feats.shape[0]
    who = [ids[k : k + 1, :] for k in range(2)]
    e_iota = lax.broadcasted_iota(jnp.int32, (experts, tokens), 0)
    named = [(e_iota == who[k]).astype(jnp.float32) for k in range(2)]
    before = lax.broadcasted_iota(jnp.int32, (tokens, tokens), 0) < lax.broadcasted_iota(jnp.int32, (tokens, tokens), 1)
    earlier = jnp.dot(
        (named[0] + named[1]).astype(jnp.bfloat16),
        jnp.where(before, 1.0, 0.0).astype(jnp.bfloat16),
        preferred_element_type=jnp.float32,
    )
    ranks = [
        jnp.sum(earlier * named[0], axis=0, keepdims=True).astype(jnp.int32),
        jnp.sum((earlier + named[0]) * named[1], axis=0, keepdims=True).astype(jnp.int32),
    ]
    row = lax.broadcasted_iota(jnp.int32, (experts * MAIN, tokens), 0)
    sub = lax.broadcasted_iota(jnp.int32, (experts * MAIN, quarter), 0) % MAIN // TAIL

    def gather(codes, wanted):
        hits = [codes[k] == wanted for k in range(2)]
        pick = jnp.where(hits[0] | hits[1], 1.0, 0.0).astype(jnp.bfloat16)
        scale = jnp.where(hits[0], probs[0:1, :], 0.0) + jnp.where(hits[1], probs[1:2, :], 0.0)
        scale = jnp.sum(scale, axis=1, keepdims=True)
        return jnp.dot(pick, feats[...], preferred_element_type=jnp.float32), scale

    got, scale = gather([jnp.where(ranks[k] < MAIN, who[k] * MAIN + ranks[k], -1) for k in range(2)], row)
    routed[:, :, 0:width] = (got * scale).astype(jnp.bfloat16).reshape(experts, MAIN, width)
    got, scale = gather(
        [jnp.where(ranks[k] >= MAIN, who[k] * TAIL + ranks[k] - MAIN, -1) for k in range(2)],
        row // MAIN * TAIL + row % TAIL,
    )
    tail = jnp.zeros((experts * MAIN, quarter), jnp.float32)
    for q in range(4):
        tail = tail + jnp.where(sub == q, got[:, q * quarter : (q + 1) * quarter], 0.0)
    routed[:, :, width : width + quarter] = (tail * scale).astype(jnp.bfloat16).reshape(experts, MAIN, quarter)

    pl.semaphore_wait(barrier, len(partners))

    def a_copy(i, other):
        target = (c + i) % yc
        source = routed.at[((1 - zh) if other else zh) * yc + target]
        return pltpu.make_async_remote_copy(
            src_ref=source,
            dst_ref=passing.at[j, c] if other else rows.at[p, x, c],
            send_sem=a_send.at[other, i],
            recv_sem=a_recv.at[other, i],
            device_id=at_c(i),
            device_id_type=MESH,
        )

    def a_arrived(i, other):
        origin = (c + yc - i) % yc
        place = passing.at[j, origin] if other else rows.at[p, x, origin]
        pltpu.make_async_copy(place, place, a_recv.at[other, i]).wait()

    for other in range(2):
        for i in range(1, yc):
            a_copy(i, other).start()
    rows[p, x, c] = routed[zh * yc + c]
    passing[j, c] = routed[(1 - zh) * yc + c]

    def unit_of(way, step):
        return (p + (step if way else -step) + ring) % ring

    def along(way):
        return zl - 1 - j if way else j

    def z_copy(way, step):
        place = rows.at[unit_of(way, step), x]
        return pltpu.make_async_remote_copy(
            src_ref=place,
            dst_ref=place,
            send_sem=z_send.at[way, step],
            recv_sem=z_recv.at[way, step + 1],
            device_id=at_ring(p + (-1 if way else 1)),
            device_id_type=MESH,
        )

    def z_arrived(way, step):
        place = rows.at[unit_of(way, step), x]
        pltpu.make_async_copy(place, place, z_recv.at[way, step]).wait()

    def t_place(way, step):
        return passing.at[(j + (step if way else -step) + zl) % zl]

    def t_copy(way, step, leaves):
        return pltpu.make_async_remote_copy(
            src_ref=t_place(way, step),
            dst_ref=rows.at[unit_of(way, step), x] if leaves else t_place(way, step),
            send_sem=t_send.at[way, step],
            recv_sem=(z_recv if leaves else t_recv).at[way, step + 1],
            device_id=at_ring(p + (-1 if way else 1)),
            device_id_type=MESH,
        )

    def t_arrived(way, step):
        place = t_place(way, step)
        pltpu.make_async_copy(place, place, t_recv.at[way, step]).wait()

    def z_forward(way, step):
        q = along(way)

        @pl.when((q < zl - 1) & (step <= q + half))
        def _():
            z_copy(way, step).start()

        @pl.when((q < zl - 1) & (step <= q - half))
        def _():
            t_copy(way, step, False).start()

        @pl.when((q == zl - 1) & (step <= q - half))
        def _():
            t_copy(way, step, True).start()

    def z_round(step):
        for way in range(2):
            q = along(way)

            @pl.when(step <= q + half)
            def _():
                z_arrived(way, step)

            @pl.when(step <= q - half)
            def _():
                t_arrived(way, step)

            z_forward(way, step)

    up, down = j + half, zl - 1 - j + half
    both = jnp.minimum(up, down)

    def unit_at(m):
        paired = m <= 2 * both
        step = jnp.where(paired, (m + 1) // 2, m - both)
        goes_up = jnp.where(paired, m % 2 == 1, up > down)
        return (p + jnp.where(goes_up, -step, step) + ring) % ring

    def x_copy(way, unit):
        place = rows.at[unit, x]
        return pltpu.make_async_remote_copy(
            src_ref=place,
            dst_ref=place,
            send_sem=x_send.at[way, unit],
            recv_sem=x_recv.at[way, unit],
            device_id=at_x(-1 if way else 1),
            device_id_type=MESH,
        )

    def x_arrived(way, unit):
        place = rows.at[unit, (x + (1 if way else dp - 1)) % dp]
        pltpu.make_async_copy(place, place, x_recv.at[way, unit]).wait()

    part = yc // 2

    def f_copy(way, unit):
        place = rows.at[unit, (x + (1 if way else dp - 1)) % dp, pl.ds(part * way, part)]
        return pltpu.make_async_remote_copy(
            src_ref=place,
            dst_ref=place,
            send_sem=f_send.at[way, unit],
            recv_sem=f_recv.at[way, unit],
            device_id=at_x(-1 if way else 1),
            device_id_type=MESH,
        )

    def f_arrived(way, unit):
        place = rows.at[unit, (x + 2) % dp, pl.ds(part * way, part)]
        pltpu.make_async_copy(place, place, f_recv.at[way, unit]).wait()

    def work(unit):
        for way in range(2):
            f_arrived(way, unit)
        zone = unit // zl
        cols = pl.ds(pl.multiple_of(unit % zl * width, width), width)
        w = held_w[:, cols]
        contract = (((1,), (1,)), ((), ()))
        count = dp * yc * MAIN
        whole = rows[unit, :, :, :, 0:width].reshape(count, width)
        acc[zone] += lax.dot_general(whole, w, contract, preferred_element_type=jnp.float32)
        quarters = rows[unit, :, :, :, width : width + quarter].reshape(count, quarter)
        of = lax.broadcasted_iota(jnp.int32, (count, quarter), 0) % MAIN // TAIL
        spread = jnp.concatenate(
            [jnp.where(of == q, quarters, jnp.zeros_like(quarters)) for q in range(4)], axis=1
        )
        acc_tail[zone] += lax.dot_general(spread, w, contract, preferred_element_type=jnp.float32)

    acc[...] = jnp.zeros_like(acc)
    acc_tail[...] = jnp.zeros_like(acc_tail)
    for i in range(1, yc):
        a_arrived(i, 0)
    for way in range(2):
        @pl.when(along(way) < zl - 1)
        def _():
            z_copy(way, 0).start()
    for way in range(2):
        x_copy(way, p).start()
    for i in range(1, yc):
        a_arrived(i, 1)
    for way in range(2):
        @pl.when((along(way) < zl - 1) & (along(way) >= half))
        def _():
            t_copy(way, 0, False).start()

        @pl.when(along(way) == zl - 1)
        def _():
            t_copy(way, 0, True).start()
    w_copy.wait()
    z_round(1)
    for way in range(2):
        x_copy(way, unit_at(1)).start()

    def turn(r, carry):
        @pl.when(r + 2 < ring)
        def _():
            for way in range(2):
                x_copy(way, unit_at(r + 2)).start()

        for way in range(2):
            x_arrived(way, unit_at(r))
            f_copy(way, unit_at(r)).start()
        z_round(r + 2)

        @pl.when(r >= 2)
        def _():
            work(unit_at(r - 2))

        return carry

    lax.fori_loop(0, ring, turn, 0)
    work(unit_at(ring - 2))
    work(unit_at(ring - 1))

    slots = MAIN + TAIL
    take = yc * MAIN
    out_row = lax.broadcasted_iota(jnp.int32, (yc * slots, yc * (MAIN + 8)), 0)
    in_row = lax.broadcasted_iota(jnp.int32, (yc * slots, yc * (MAIN + 8)), 1)
    group, slot = out_row // slots, out_row % slots
    source = jnp.where(slot < MAIN, group * MAIN + slot, take + group * 8 + slot - MAIN)
    place = jnp.where(source == in_row, 1.0, 0.0).astype(jnp.bfloat16)
    for zone in range(2):
        for at in range(dp):
            main = acc[zone, pl.ds(at * take, take), :].astype(jnp.bfloat16)
            ends = acc_tail[zone, pl.ds(at * take, take), :].reshape(yc, MAIN, acc.shape[-1])
            ends = ends[:, 0:8, :] + ends[:, 8:16, :]
            ends = ends.reshape(yc * 8, acc.shape[-1])
            turned = pltpu.roll(ends, yc * 8 - TAIL, 0)
            ends = (ends + turned).astype(jnp.bfloat16)
            done = jnp.dot(place, jnp.concatenate([main, ends], axis=0), preferred_element_type=jnp.float32)
            start = (at * 2 + zone) * yc * slots
            out[0, pl.ds(start, yc * slots), :] = done.astype(jnp.bfloat16)

    for other in range(2):
        for i in range(1, yc):
            a_copy(i, other).wait_send()

    def left(step, carry):
        for way in range(2):
            q = along(way)

            @pl.when((q < zl - 1) & (step <= q + half))
            def _():
                z_copy(way, step).wait_send()

            @pl.when(step <= q - half)
            def _():
                t_copy(way, step, False).wait_send()

            x_copy(way, step).wait_send()
            f_copy(way, step).wait_send()
        return carry

    lax.fori_loop(0, ring, left, 0)


def body(layer_grad, gate_probs, expert_ids, down_weight):
    dp, zl = lax.axis_size("dp"), lax.axis_size("tensor")
    experts = down_weight.shape[0] * lax.axis_size("expert")
    yc = experts // 2
    ring = 2 * zl
    width = layer_grad.shape[1]
    hidden = down_weight.shape[1]
    half = zl // 2
    chunk = (MAIN, width + width // 4)
    count = dp * yc * MAIN
    dma = pltpu.SemaphoreType.DMA
    steps = zl + half + 1
    vmem = pl.BlockSpec(memory_space=pltpu.VMEM)
    total = dp * experts * (MAIN + TAIL)
    return pl.pallas_call(
        functools.partial(kernel, (dp, yc, zl, width)),
        out_shape=jax.ShapeDtypeStruct((1, total, hidden), jnp.bfloat16),
        in_specs=[vmem, vmem, vmem, pl.BlockSpec(memory_space=pl.ANY)],
        out_specs=vmem,
        scratch_shapes=[
            pltpu.VMEM((experts, *chunk), jnp.bfloat16),
            pltpu.VMEM((ring, dp, yc, *chunk), jnp.bfloat16),
            pltpu.VMEM((zl, yc, *chunk), jnp.bfloat16),
            pltpu.VMEM(down_weight.shape[1:], jnp.bfloat16),
            pltpu.VMEM((2, count, hidden), jnp.float32),
            pltpu.VMEM((2, count, hidden), jnp.float32),
            dma,
            dma((2, yc)), dma((2, yc)),
            dma((2, steps)), dma((2, steps)),
            dma((2, half + 1)), dma((2, half + 1)),
            dma((2, ring)), dma((2, ring)),
            dma((2, ring)), dma((2, ring)),
        ],
        compiler_params=pltpu.CompilerParams(
            collective_id=0, has_side_effects=True, vmem_limit_bytes=48 * 1024 * 1024
        ),
        cost_estimate=pl.CostEstimate(
            flops=2 * total * hidden * width * zl,
            bytes_accessed=2 * (down_weight.size + total * hidden),
            transcendentals=0,
        ),
    )(layer_grad, gate_probs.T, expert_ids.T, down_weight)


def solution(mesh):
    placed = (
        P(("dp", "expert"), "tensor"),
        P(("dp", "expert"), None),
        P(("dp", "expert"), None),
        P("expert", ("dp", "tensor"), None),
    )
    return jax.shard_map(
        body,
        mesh=mesh,
        in_specs=placed,
        out_specs=P("expert", None, ("dp", "tensor")),
        check_vma=False,
    )
```

time: 256 us -> 120 us (0.47)
  the two profiles are of different devices: /device:TPU:1 before, /device:TPU:2 now
where the time goes in v1:
time: 120 us
  Pallas kernels  115 us (96%)
  local copies, waits for them, and re-layouts  5.1 us (4%)
    pallas_call x1, Pallas kernels, body(): pl.pallas_call(functools.partial(kernel, (dp, yc, zl, width)), out_shape=...  115 us
    unnamed x9, local copies, waits for them, and re-layouts  5.1 us

profile of v1, /device:TPU:2, one launch (start us, length us, event | category | flops | bytes accessed | tf_op | source)
XLA Modules:
  0.0 119.7 jit_solution(6968006093455153741)
XLA Ops:
  0.0 0.0 copy-start
  0.0 1.9 %copy-done = bf16[1,384,4096]{2,1,0:T(8,128)(2,1)S(1)} copy-done((bf16[1,384,4096]{2,1,0:T(8,128)(2,1)S(1)}, bf16[1,384,4096]{2,1,0:T(8,128)(2,1)}, u32[]{:S(2)}) %copy-start) | copy-done | bytes 3145752
  1.9 0.0 copy-start.1
  1.9 0.9 copy-done.1
  2.8 0.0 copy-start.2
  2.8 0.7 copy-done.2
  3.5 0.0 copy-start.3
  3.5 0.7 copy-done.3
  4.2 114.6 %shard_map.46 = bf16[1,1280,384]{2,1,0:T(8,128)(2,1)S(1)} custom-call(bf16[128,512]{1,0:T(8,128)(2,1)S(1)} %copy-done.1, f32[2,128]{1,0:T(2,128)S(1)} %bitcast.2, s32[2,128]{1,0:T(2,128)S(1)} %bitcast.3, bf16[1,384,4096]{2,1,0:T(8,128)(2,1)S(1)} %copy-done), custom_call_target="tpu_custom_call" | custom-call | flops 4026531840 | bytes 4128768 | tf_op jit(solution)/shard_map/pallas_call | solution.py:337
  118.8 0.9 copy.6
Async XLA Ops:
  0.0 1.9 %copy-start = (bf16[1,384,4096]{2,1,0:T(8,128)(2,1)S(1)}, bf16[1,384,4096]{2,1,0:T(8,128)(2,1)}, u32[]{:S(2)}) copy-start(bf16[1,384,4096]{2,1,0:T(8,128)(2,1)} %weight.1) | copy-start | bytes 9437188
  1.9 0.9 copy-start.1
  2.8 0.7 copy-start.2
  3.5 0.7 copy-start.3

commit v2 on v1

v2 whole, which is shorter than its diff:
```python
import functools

import jax
import jax.numpy as jnp
from jax import lax
from jax.experimental import pallas as pl
from jax.experimental.pallas import tpu as pltpu
from jax.sharding import PartitionSpec as P

MESH = pl.DeviceIdType.MESH
MAIN = 16
TAIL = 4


def kernel(
    shape,
    feats_in, probs_in, ids_in, weight, out,
    feats, probs, ids, in_sem, routed, rows, passing, weights, acc, sums_out, sums_in, w_sem,
    a_send, a_recv, z_send, z_recv, t_send, t_recv, x_send, x_recv, v_send, v_recv, s_send, s_recv,
):
    dp, yc, zl, width = shape
    half = zl // 2
    ring = 2 * zl
    quarter = width // 4
    experts = 2 * yc
    x = lax.axis_index("dp")
    ex = lax.axis_index("expert")
    j = lax.axis_index("tensor")
    zh, c = ex // yc, ex % yc
    p = zh * zl + j

    def at_ring(pos):
        pos = (pos + ring) % ring
        return {"expert": (pos // zl) * yc + c, "tensor": pos % zl}

    def at_x(offset):
        return {"dp": (x + offset + dp) % dp}

    def at_c(offset):
        return {"expert": zh * yc + (c + offset) % yc}

    loads = [
        pltpu.make_async_copy(source, target, in_sem.at[i])
        for i, (source, target) in enumerate([(ids_in, ids), (probs_in, probs), (feats_in, feats)])
    ]
    for load in loads:
        load.start()
    barrier = pltpu.get_barrier_semaphore()
    partners = [at_ring(p + 1), at_ring(p - 1), at_x(1), at_x(-1)] + [at_c(i) for i in range(1, yc)]
    for partner in partners:
        pl.semaphore_signal(barrier, inc=1, device_id=partner, device_id_type=MESH)

    hidden = weight.shape[1]
    w_copies = [
        pltpu.make_async_copy(
            weight.at[0, :, pl.ds(s * width, width)], weights.at[s, pl.ds(0, hidden)], w_sem.at[s]
        )
        for s in range(zl)
    ]
    for w_copy in w_copies:
        w_copy.start()

    for load in loads:
        load.wait()
    tokens = feats.shape[0]
    who = [ids[k : k + 1, :] for k in range(2)]
    e_iota = lax.broadcasted_iota(jnp.int32, (experts, tokens), 0)
    named = [(e_iota == who[k]).astype(jnp.float32) for k in range(2)]
    before = lax.broadcasted_iota(jnp.int32, (tokens, tokens), 0) < lax.broadcasted_iota(jnp.int32, (tokens, tokens), 1)
    earlier = jnp.dot(
        (named[0] + named[1]).astype(jnp.bfloat16),
        jnp.where(before, 1.0, 0.0).astype(jnp.bfloat16),
        preferred_element_type=jnp.float32,
    )
    ranks = [
        jnp.sum(earlier * named[0], axis=0, keepdims=True).astype(jnp.int32),
        jnp.sum((earlier + named[0]) * named[1], axis=0, keepdims=True).astype(jnp.int32),
    ]
    row = lax.broadcasted_iota(jnp.int32, (experts * MAIN, tokens), 0)
    sub = lax.broadcasted_iota(jnp.int32, (experts * MAIN, quarter), 0) % MAIN // TAIL

    def gather(codes, wanted):
        hits = [codes[k] == wanted for k in range(2)]
        pick = jnp.where(hits[0] | hits[1], 1.0, 0.0).astype(jnp.bfloat16)
        scale = jnp.where(hits[0], probs[0:1, :], 0.0) + jnp.where(hits[1], probs[1:2, :], 0.0)
        scale = jnp.sum(scale, axis=1, keepdims=True)
        return jnp.dot(pick, feats[...], preferred_element_type=jnp.float32), scale

    got, scale = gather([jnp.where(ranks[k] < MAIN, who[k] * MAIN + ranks[k], -1) for k in range(2)], row)
    routed[:, :, 0:width] = (got * scale).astype(jnp.bfloat16).reshape(experts, MAIN, width)
    got, scale = gather(
        [jnp.where(ranks[k] >= MAIN, who[k] * TAIL + ranks[k] - MAIN, -1) for k in range(2)],
        row // MAIN * TAIL + row % TAIL,
    )
    tail = jnp.zeros((experts * MAIN, quarter), jnp.float32)
    for q in range(4):
        tail = tail + jnp.where(sub == q, got[:, q * quarter : (q + 1) * quarter], 0.0)
    routed[:, :, width : width + quarter] = (tail * scale).astype(jnp.bfloat16).reshape(experts, MAIN, quarter)

    pl.semaphore_wait(barrier, len(partners))

    def beside(parity):
        return jnp.where((x + parity) % 2 == 0, -1, 1)

    def v_copy(s):
        return pltpu.make_async_remote_copy(
            src_ref=weights.at[s, pl.ds(0, hidden)],
            dst_ref=weights.at[s, pl.ds(hidden, hidden)],
            send_sem=v_send.at[s],
            recv_sem=v_recv.at[s],
            device_id=at_x(beside(1 - s % 2)),
            device_id_type=MESH,
        )

    for s in range(zl):
        w_copies[s].wait()
        v_copy(s).start()

    def a_copy(i, other):
        target = (c + i) % yc
        source = routed.at[((1 - zh) if other else zh) * yc + target]
        return pltpu.make_async_remote_copy(
            src_ref=source,
            dst_ref=passing.at[j, c] if other else rows.at[p, 0, c],
            send_sem=a_send.at[other, i],
            recv_sem=a_recv.at[other, i],
            device_id=at_c(i),
            device_id_type=MESH,
        )

    def a_arrived(i, other):
        origin = (c + yc - i) % yc
        place = passing.at[j, origin] if other else rows.at[p, 0, origin]
        pltpu.make_async_copy(place, place, a_recv.at[other, i]).wait()

    piece = yc // 2

    def unit_of(way, step):
        return (p + (step if way else -step) + ring) % ring

    def along(way):
        return zl - 1 - j if way else j

    def z_place(way, step, h):
        return rows.at[unit_of(way, step), 0, pl.ds(h * piece, piece)]

    def t_place(way, step, h):
        return passing.at[(j + (step if way else -step) + zl) % zl, pl.ds(h * piece, piece)]

    def z_copy(way, step, h):
        return pltpu.make_async_remote_copy(
            src_ref=z_place(way, step, h),
            dst_ref=z_place(way, step, h),
            send_sem=z_send.at[way, step, h],
            recv_sem=z_recv.at[way, step + 1, h],
            device_id=at_ring(p + (-1 if way else 1)),
            device_id_type=MESH,
        )

    def t_copy(way, step, h, leaves):
        return pltpu.make_async_remote_copy(
            src_ref=t_place(way, step, h),
            dst_ref=(z_place if leaves else t_place)(way, step, h),
            send_sem=t_send.at[way, step, h],
            recv_sem=(z_recv if leaves else t_recv).at[way, step + 1, h],
            device_id=at_ring(p + (-1 if way else 1)),
            device_id_type=MESH,
        )

    def z_start(way, step, h):
        @pl.when((along(way) < zl - 1) & (step <= along(way) + half))
        def _():
            z_copy(way, step, h).start()

    def t_start(way, step, h):
        q = along(way)

        @pl.when((q < zl - 1) & (step <= q - half))
        def _():
            t_copy(way, step, h, False).start()

        @pl.when((q == zl - 1) & (step <= q - half))
        def _():
            t_copy(way, step, h, True).start()

    def x_copy(unit):
        return pltpu.make_async_remote_copy(
            src_ref=rows.at[unit, 0],
            dst_ref=rows.at[unit, 1],
            send_sem=x_send.at[unit],
            recv_sem=x_recv.at[unit],
            device_id=at_x(beside(unit % 2)),
            device_id_type=MESH,
        )

    def z_round(step):
        for h in range(2):
            for way in range(2):
                @pl.when(step <= along(way) + half)
                def _():
                    place = z_place(way, step, h)
                    pltpu.make_async_copy(place, place, z_recv.at[way, step, h]).wait()

                z_start(way, step, h)

                @pl.when(step <= along(way) - half)
                def _():
                    place = t_place(way, step, h)
                    pltpu.make_async_copy(place, place, t_recv.at[way, step, h]).wait()

                t_start(way, step, h)
        for way in range(2):
            @pl.when(step <= along(way) + half)
            def _():
                x_copy(unit_of(way, step)).start()

    up, down = j + half, zl - 1 - j + half
    both = jnp.minimum(up, down)

    def unit_at(m):
        paired = m <= 2 * both
        step = jnp.where(paired, (m + 1) // 2, m - both)
        goes_up = jnp.where(paired, m % 2 == 1, up > down)
        return (p + jnp.where(goes_up, -step, step) + ring) % ring

    count = yc * MAIN

    def work(unit):
        place = rows.at[unit, 1]
        pltpu.make_async_copy(place, place, x_recv.at[unit]).wait()
        zone, s = unit // zl, unit % zl
        w = weights[s]
        contract = (((1,), (1,)), ((), ()))
        whole = rows[unit, :, :, :, 0:width].reshape(2 * count, width)
        acc[s % 2, zone, 0] += lax.dot_general(whole, w, contract, preferred_element_type=jnp.float32)
        quarters = rows[unit, :, :, :, width : width + quarter].reshape(2 * count, quarter)
        of = lax.broadcasted_iota(jnp.int32, (2 * count, quarter), 0) % MAIN // TAIL
        spread = jnp.concatenate(
            [jnp.where(of == q, quarters, jnp.zeros_like(quarters)) for q in range(4)], axis=1
        )
        acc[s % 2, zone, 1] += lax.dot_general(spread, w, contract, preferred_element_type=jnp.float32)

    slots = MAIN + TAIL
    out_row = lax.broadcasted_iota(jnp.int32, (yc * slots, yc * (MAIN + 8)), 0)
    in_row = lax.broadcasted_iota(jnp.int32, (yc * slots, yc * (MAIN + 8)), 1)
    group, slot = out_row // slots, out_row % slots
    source = jnp.where(slot < MAIN, group * MAIN + slot, count + group * 8 + slot - MAIN)
    order = jnp.where(source == in_row, 1.0, 0.0).astype(jnp.bfloat16)

    def in_order(main, ends):
        ends = ends.reshape(yc, MAIN, ends.shape[-1])
        ends = (ends[:, 0:8, :] + ends[:, 8:16, :]).reshape(yc * 8, ends.shape[-1])
        ends = ends + pltpu.roll(ends, yc * 8 - TAIL, 0)
        both_parts = jnp.concatenate([main.astype(jnp.bfloat16), ends.astype(jnp.bfloat16)], axis=0)
        return jnp.dot(order, both_parts, preferred_element_type=jnp.float32)

    def s_copy(parity, zone):
        return pltpu.make_async_remote_copy(
            src_ref=sums_out.at[parity, zone],
            dst_ref=sums_in.at[parity, zone],
            send_sem=s_send.at[parity, zone],
            recv_sem=s_recv.at[parity, zone],
            device_id=at_x(beside(1 - parity)),
            device_id_type=MESH,
        )

    def give(zone):
        for parity in range(2):
            for col in range(2):
                at = pl.ds(col * count, count)
                theirs = pl.ds(hidden, hidden)
                part = in_order(acc[parity, zone, 0, at, theirs], acc[parity, zone, 1, at, theirs])
                sums_out[parity, zone, col] = part.astype(jnp.bfloat16)
            s_copy(parity, zone).start()

    def store(column, zone, value):
        start = pl.multiple_of((column * 2 + zone) * yc * slots, MAIN)
        out[0, pl.ds(start, yc * slots), :] = value.astype(jnp.bfloat16)

    def finish(zone):
        mine = pl.ds(0, hidden)
        own, next_to = pl.ds(0, count), pl.ds(count, count)
        store(x, zone, in_order(
            acc[0, zone, 0, own, mine] + acc[1, zone, 0, own, mine],
            acc[0, zone, 1, own, mine] + acc[1, zone, 1, own, mine],
        ))
        local = [in_order(acc[k, zone, 0, next_to, mine], acc[k, zone, 1, next_to, mine]) for k in range(2)]
        for parity in range(2):
            place = sums_in.at[parity, zone]
            pltpu.make_async_copy(place, place, s_recv.at[parity, zone]).wait()
        for parity in range(2):
            column = (x + beside(parity) + dp) % dp
            store(column, zone, local[parity] + sums_in[1 - parity, zone, 0].astype(jnp.float32))
        store((x + 2) % dp, zone, sums_in[0, zone, 1].astype(jnp.float32) + sums_in[1, zone, 1].astype(jnp.float32))

    for other in range(2):
        for i in range(1, yc):
            a_copy(i, other).start()
    rows[p, 0, c] = routed[zh * yc + c]
    passing[j, c] = routed[(1 - zh) * yc + c]
    acc[...] = jnp.zeros_like(acc)
    for i in range(1, yc):
        a_arrived(i, 0)
    for h in range(2):
        for way in range(2):
            z_start(way, 0, h)
    x_copy(p).start()
    for i in range(1, yc):
        a_arrived(i, 1)
    for h in range(2):
        for way in range(2):
            t_start(way, 0, h)

    late = half + 1

    def turn(r, carry):
        z_round(r + 1)

        @pl.when(r == late)
        def _():
            for s in range(zl):
                place = weights.at[s, pl.ds(hidden, hidden)]
                pltpu.make_async_copy(place, place, v_recv.at[s]).wait()

        @pl.when(r >= late)
        def _():
            work(unit_at(2 * (r - late)))
            work(unit_at(2 * (r - late) + 1))

        @pl.when(r == late + (zl - 1 + half) // 2)
        def _():
            give(zh)

        return carry

    lax.fori_loop(0, late + zl, turn, 0)
    give(1 - zh)
    finish(zh)
    finish(1 - zh)

    for other in range(2):
        for i in range(1, yc):
            a_copy(i, other).wait_send()
    for s in range(zl):
        v_copy(s).wait_send()
    for parity in range(2):
        for zone in range(2):
            s_copy(parity, zone).wait_send()

    def left(step, carry):
        for way in range(2):
            q = along(way)
            for h in range(2):
                @pl.when((q < zl - 1) & (step <= q + half))
                def _():
                    z_copy(way, step, h).wait_send()

                @pl.when(step <= q - half)
                def _():
                    t_copy(way, step, h, False).wait_send()

        x_copy(step).wait_send()
        return carry

    lax.fori_loop(0, ring, left, 0)


def body(layer_grad, gate_probs, expert_ids, down_weight):
    dp, zl = lax.axis_size("dp"), lax.axis_size("tensor")
    experts = down_weight.shape[0] * lax.axis_size("expert")
    yc = experts // 2
    ring = 2 * zl
    width = layer_grad.shape[1]
    hidden = down_weight.shape[1]
    half = zl // 2
    chunk = (MAIN, width + width // 4)
    dma = pltpu.SemaphoreType.DMA
    steps = zl + half + 1
    vmem = pl.BlockSpec(memory_space=pltpu.VMEM)
    total = dp * experts * (MAIN + TAIL)
    return pl.pallas_call(
        functools.partial(kernel, (dp, yc, zl, width)),
        out_shape=jax.ShapeDtypeStruct((1, total, hidden), jnp.bfloat16),
        in_specs=[pl.BlockSpec(memory_space=pl.ANY)] * 4,
        out_specs=vmem,
        scratch_shapes=[
            pltpu.VMEM(layer_grad.shape, jnp.bfloat16),
            pltpu.VMEM((2, layer_grad.shape[0]), jnp.float32),
            pltpu.VMEM((2, layer_grad.shape[0]), jnp.int32),
            dma((3,)),
            pltpu.VMEM((experts, *chunk), jnp.bfloat16),
            pltpu.VMEM((ring, 2, yc, *chunk), jnp.bfloat16),
            pltpu.VMEM((zl, yc, *chunk), jnp.bfloat16),
            pltpu.VMEM((zl, 2 * hidden, width), jnp.bfloat16),
            pltpu.VMEM((2, 2, 2, 2 * yc * MAIN, 2 * hidden), jnp.float32),
            pltpu.VMEM((2, 2, 2, yc * (MAIN + TAIL), hidden), jnp.bfloat16),
            pltpu.VMEM((2, 2, 2, yc * (MAIN + TAIL), hidden), jnp.bfloat16),
            dma((zl,)),
            dma((2, yc)), dma((2, yc)),
            dma((2, steps, 2)), dma((2, steps, 2)),
            dma((2, half + 1, 2)), dma((2, half + 1, 2)),
            dma((ring,)), dma((ring,)),
            dma((zl,)), dma((zl,)),
            dma((2, 2)), dma((2, 2)),
        ],
        compiler_params=pltpu.CompilerParams(
            collective_id=0, has_side_effects=True, vmem_limit_bytes=62 * 1024 * 1024
        ),
        cost_estimate=pl.CostEstimate(
            flops=2 * total * hidden * width * zl,
            bytes_accessed=2 * (down_weight.size + total * hidden),
            transcendentals=0,
        ),
    )(layer_grad, gate_probs.T, expert_ids.T, down_weight)


def solution(mesh):
    placed = (
        P(("dp", "expert"), "tensor"),
        P(("dp", "expert"), None),
        P(("dp", "expert"), None),
        P("expert", ("dp", "tensor"), None),
    )
    return jax.shard_map(
        body,
        mesh=mesh,
        in_specs=placed,
        out_specs=P("expert", None, ("dp", "tensor")),
        check_vma=False,
    )
```

time: 120 us -> 92 us (0.77)
  the two profiles are of different devices: /device:TPU:2 before, /device:TPU:1 now
where the time goes in v2:
time: 92 us; the launch traced here: 91.8 us
  Pallas kernels  89.6 us (97%)
  local copies, waits for them, and re-layouts  2.24 us (2%)
    pallas_call x1, Pallas kernels, body(): pl.pallas_call(functools.partial(kernel, (dp, yc, zl, width)), out_shape=...  89.6 us
    unnamed x1, local copies, waits for them, and re-layouts  2.24 us

profile of v2, /device:TPU:1, one launch (start us, length us, event | category | flops | bytes accessed | tf_op | source)
XLA Modules:
  0.0 91.8 jit_solution(3255670725710967783)
XLA Ops:
  0.0 89.6 %shard_map.46 = bf16[1,1280,384]{2,1,0:T(8,128)(2,1)} custom-call(bf16[128,512]{1,0:T(8,128)(2,1)} %feats_in.1, f32[2,128]{1,0:T(2,128)} %bitcast.2, s32[2,128]{1,0:T(2,128)} %bitcast.3, bf16[1,384,4096]{2,1,0:T(8,128)(2,1)} %weight.1), custom_call_target="tpu_custom_call" | custom-call | flops 4026531840 | bytes 4128768 | tf_op jit(solution)/shard_map/pallas_call | solution.py:381
  89.6 2.2 %copy.6 = bf16[1,1280,384]{2,1,0:T(8,128)(2,1)} copy(bf16[1,1280,384]{2,1,0:T(8,128)(2,1)} %shard_map.46) | data formatting | bytes 1966080

commit v3 on v2

--- a/solution.py
+++ b/solution.py
@@ -45,6 +45,19 @@
     ]
     for load in loads:
         load.start()
+    short, long = jnp.minimum(j, zl - 1 - j), jnp.maximum(j, zl - 1 - j)
+    long_up = j > zl - 1 - j
+
+    def unit_at(m):
+        paired = m <= 2 * short
+        native = m < zl
+        step = jnp.where(paired, (m + 1) // 2, m - short)
+        goes_up = jnp.where(paired, m % 2 == 1, long_up)
+        far = m - zl
+        step = jnp.where(native, step, jnp.where(far < half, short + 1 + far, long + 1 + far - half))
+        goes_up = jnp.where(native, goes_up, jnp.where(far < half, ~long_up, long_up))
+        return (p + jnp.where(goes_up, -step, step) + ring) % ring
+
     barrier = pltpu.get_barrier_semaphore()
     partners = [at_ring(p + 1), at_ring(p - 1), at_x(1), at_x(-1)] + [at_c(i) for i in range(1, yc)]
     for partner in partners:
@@ -88,6 +101,25 @@
 
     got, scale = gather([jnp.where(ranks[k] < MAIN, who[k] * MAIN + ranks[k], -1) for k in range(2)], row)
     routed[:, :, 0:width] = (got * scale).astype(jnp.bfloat16).reshape(experts, MAIN, width)
+    pl.semaphore_wait(barrier, len(partners))
+
+    beside = jnp.where((x + c) % 2 == 0, -1, 1)
+
+    def v_copy(s):
+        return pltpu.make_async_remote_copy(
+            src_ref=weights.at[s, pl.ds(0, hidden)],
+            dst_ref=weights.at[s, pl.ds(hidden, hidden)],
+            send_sem=v_send.at[s],
+            recv_sem=v_recv.at[s],
+            device_id=at_x(-beside),
+            device_id_type=MESH,
+        )
+
+    for s in range(zl):
+        w_copies[s].wait()
+    for m in range(zl):
+        v_copy(unit_at(m) % zl).start()
+
     got, scale = gather(
         [jnp.where(ranks[k] >= MAIN, who[k] * TAIL + ranks[k] - MAIN, -1) for k in range(2)],
         row // MAIN * TAIL + row % TAIL,
@@ -97,25 +129,6 @@
         tail = tail + jnp.where(sub == q, got[:, q * quarter : (q + 1) * quarter], 0.0)
     routed[:, :, width : width + quarter] = (tail * scale).astype(jnp.bfloat16).reshape(experts, MAIN, quarter)
 
-    pl.semaphore_wait(barrier, len(partners))
-
-    def beside(parity):
-        return jnp.where((x + parity) % 2 == 0, -1, 1)
-
-    def v_copy(s):
-        return pltpu.make_async_remote_copy(
-            src_ref=weights.at[s, pl.ds(0, hidden)],
-            dst_ref=weights.at[s, pl.ds(hidden, hidden)],
-            send_sem=v_send.at[s],
-            recv_sem=v_recv.at[s],
-            device_id=at_x(beside(1 - s % 2)),
-            device_id_type=MESH,
-        )
-
-    for s in range(zl):
-        w_copies[s].wait()
-        v_copy(s).start()
-
     def a_copy(i, other):
         target = (c + i) % yc
         source = routed.at[((1 - zh) if other else zh) * yc + target]
@@ -183,13 +196,13 @@
         def _():
             t_copy(way, step, h, True).start()
 
-    def x_copy(unit):
-        return pltpu.make_async_remote_copy(
-            src_ref=rows.at[unit, 0],
-            dst_ref=rows.at[unit, 1],
-            send_sem=x_send.at[unit],
-            recv_sem=x_recv.at[unit],
-            device_id=at_x(beside(unit % 2)),
+    def x_copy(unit, h):
+        return pltpu.make_async_remote_copy(
+            src_ref=rows.at[unit, 0, pl.ds(h * piece, piece)],
+            dst_ref=rows.at[unit, 1, pl.ds(h * piece, piece)],
+            send_sem=x_send.at[unit, h],
+            recv_sem=x_recv.at[unit, h],
+            device_id=at_x(beside),
             device_id_type=MESH,
         )
 
@@ -203,42 +216,41 @@
 
                 z_start(way, step, h)
 
+                @pl.when(step <= along(way) + half)
+                def _():
+                    x_copy(unit_of(way, step), h).start()
+
                 @pl.when(step <= along(way) - half)
                 def _():
                     place = t_place(way, step, h)
                     pltpu.make_async_copy(place, place, t_recv.at[way, step, h]).wait()
 
                 t_start(way, step, h)
-        for way in range(2):
-            @pl.when(step <= along(way) + half)
-            def _():
-                x_copy(unit_of(way, step)).start()
-
-    up, down = j + half, zl - 1 - j + half
-    both = jnp.minimum(up, down)
-
-    def unit_at(m):
-        paired = m <= 2 * both
-        step = jnp.where(paired, (m + 1) // 2, m - both)
-        goes_up = jnp.where(paired, m % 2 == 1, up > down)
-        return (p + jnp.where(goes_up, -step, step) + ring) % ring
 
     count = yc * MAIN
 
-    def work(unit):
-        place = rows.at[unit, 1]
-        pltpu.make_async_copy(place, place, x_recv.at[unit]).wait()
+    def work(m):
+        unit = unit_at(m)
+        for h in range(2):
+            place = rows.at[unit, 1, pl.ds(h * piece, piece)]
+            pltpu.make_async_copy(place, place, x_recv.at[unit, h]).wait()
         zone, s = unit // zl, unit % zl
+
+        @pl.when(m < zl)
+        def _():
+            theirs = weights.at[s, pl.ds(hidden, hidden)]
+            pltpu.make_async_copy(theirs, theirs, v_recv.at[s]).wait()
+
         w = weights[s]
         contract = (((1,), (1,)), ((), ()))
         whole = rows[unit, :, :, :, 0:width].reshape(2 * count, width)
-        acc[s % 2, zone, 0] += lax.dot_general(whole, w, contract, preferred_element_type=jnp.float32)
+        acc[zone, 0] += lax.dot_general(whole, w, contract, preferred_element_type=jnp.float32)
         quarters = rows[unit, :, :, :, width : width + quarter].reshape(2 * count, quarter)
         of = lax.broadcasted_iota(jnp.int32, (2 * count, quarter), 0) % MAIN // TAIL
         spread = jnp.concatenate(
             [jnp.where(of == q, quarters, jnp.zeros_like(quarters)) for q in range(4)], axis=1
         )
-        acc[s % 2, zone, 1] += lax.dot_general(spread, w, contract, preferred_element_type=jnp.float32)
+        acc[zone, 1] += lax.dot_general(spread, w, contract, preferred_element_type=jnp.float32)
 
     slots = MAIN + TAIL
     out_row = lax.broadcasted_iota(jnp.int32, (yc * slots, yc * (MAIN + 8)), 0)
@@ -254,44 +266,38 @@
         both_parts = jnp.concatenate([main.astype(jnp.bfloat16), ends.astype(jnp.bfloat16)], axis=0)
         return jnp.dot(order, both_parts, preferred_element_type=jnp.float32)
 
-    def s_copy(parity, zone):
-        return pltpu.make_async_remote_copy(
-            src_ref=sums_out.at[parity, zone],
-            dst_ref=sums_in.at[parity, zone],
-            send_sem=s_send.at[parity, zone],
-            recv_sem=s_recv.at[parity, zone],
-            device_id=at_x(beside(1 - parity)),
-            device_id_type=MESH,
-        )
+    def s_copy(zone, col):
+        return pltpu.make_async_remote_copy(
+            src_ref=sums_out.at[zone, col],
+            dst_ref=sums_in.at[zone, col],
+            send_sem=s_send.at[zone, col],
+            recv_sem=s_recv.at[zone, col],
+            device_id=at_x(-beside),
+            device_id_type=MESH,
+        )
+
+    def part(zone, col, cols):
+        at = pl.ds(col * count, count)
+        return in_order(acc[zone, 0, at, cols], acc[zone, 1, at, cols]).astype(jnp.bfloat16)
 
     def give(zone):
-        for parity in range(2):
-            for col in range(2):
-                at = pl.ds(col * count, count)
-                theirs = pl.ds(hidden, hidden)
-                part = in_order(acc[parity, zone, 0, at, theirs], acc[parity, zone, 1, at, theirs])
-                sums_out[parity, zone, col] = part.astype(jnp.bfloat16)
-            s_copy(parity, zone).start()
+        for col in range(2):
+            sums_out[zone, col] = part(zone, col, pl.ds(hidden, hidden))
+            s_copy(zone, col).start()
 
     def store(column, zone, value):
-        start = pl.multiple_of((column * 2 + zone) * yc * slots, MAIN)
-        out[0, pl.ds(start, yc * slots), :] = value.astype(jnp.bfloat16)
-
-    def finish(zone):
-        mine = pl.ds(0, hidden)
-        own, next_to = pl.ds(0, count), pl.ds(count, count)
-        store(x, zone, in_order(
-            acc[0, zone, 0, own, mine] + acc[1, zone, 0, own, mine],
-            acc[0, zone, 1, own, mine] + acc[1, zone, 1, own, mine],
-        ))
-        local = [in_order(acc[k, zone, 0, next_to, mine], acc[k, zone, 1, next_to, mine]) for k in range(2)]
-        for parity in range(2):
-            place = sums_in.at[parity, zone]
-            pltpu.make_async_copy(place, place, s_recv.at[parity, zone]).wait()
-        for parity in range(2):
-            column = (x + beside(parity) + dp) % dp
-            store(column, zone, local[parity] + sums_in[1 - parity, zone, 0].astype(jnp.float32))
-        store((x + 2) % dp, zone, sums_in[0, zone, 1].astype(jnp.float32) + sums_in[1, zone, 1].astype(jnp.float32))
+        start = pl.multiple_of(((column + dp) % dp * 2 + zone) * yc * slots, MAIN)
+        out[0, pl.ds(start, yc * slots), :] = value
+
+    def keep(zone):
+        for col in range(2):
+            store(x + col * beside, zone, part(zone, col, pl.ds(0, hidden)))
+
+    def take(zone):
+        for col in range(2):
+            place = sums_in.at[zone, col]
+            pltpu.make_async_copy(place, place, s_recv.at[zone, col]).wait()
+            store(x + (2 if col else -beside), zone, sums_in[zone, col])
 
     for other in range(2):
         for i in range(1, yc):
@@ -304,30 +310,26 @@
     for h in range(2):
         for way in range(2):
             z_start(way, 0, h)
-    x_copy(p).start()
+    for h in range(2):
+        x_copy(p, h).start()
     for i in range(1, yc):
         a_arrived(i, 1)
     for h in range(2):
         for way in range(2):
             t_start(way, 0, h)
 
-    late = half + 1
+    late = half + 2
 
     def turn(r, carry):
         z_round(r + 1)
 
-        @pl.when(r == late)
-        def _():
-            for s in range(zl):
-                place = weights.at[s, pl.ds(hidden, hidden)]
-                pltpu.make_async_copy(place, place, v_recv.at[s]).wait()
 
         @pl.when(r >= late)
         def _():
-            work(unit_at(2 * (r - late)))
-            work(unit_at(2 * (r - late) + 1))
-
-        @pl.when(r == late + (zl - 1 + half) // 2)
+            work(2 * (r - late))
+            work(2 * (r - late) + 1)
+
+        @pl.when(r == late + zl // 2 - 1)
         def _():
             give(zh)
 
@@ -335,17 +337,19 @@
 
     lax.fori_loop(0, late + zl, turn, 0)
     give(1 - zh)
-    finish(zh)
-    finish(1 - zh)
+    keep(zh)
+    take(zh)
+    keep(1 - zh)
+    take(1 - zh)
 
     for other in range(2):
         for i in range(1, yc):
             a_copy(i, other).wait_send()
     for s in range(zl):
         v_copy(s).wait_send()
-    for parity in range(2):
-        for zone in range(2):
-            s_copy(parity, zone).wait_send()
+    for zone in range(2):
+        for col in range(2):
+            s_copy(zone, col).wait_send()
 
     def left(step, carry):
         for way in range(2):
@@ -359,7 +363,8 @@
                 def _():
                     t_copy(way, step, h, False).wait_send()
 
-        x_copy(step).wait_send()
+        for h in range(2):
+            x_copy(step, h).wait_send()
         return carry
 
     lax.fori_loop(0, ring, left, 0)
@@ -380,8 +385,8 @@
     total = dp * experts * (MAIN + TAIL)
     return pl.pallas_call(
         functools.partial(kernel, (dp, yc, zl, width)),
-        out_shape=jax.ShapeDtypeStruct((1, total, hidden), jnp.bfloat16),
-        in_specs=[pl.BlockSpec(memory_space=pl.ANY)] * 4,
+        out_shape=pltpu.VMEM((1, total, hidden), jnp.bfloat16),
+        in_specs=[pl.BlockSpec(memory_space=pltpu.HBM)] * 4,
         out_specs=vmem,
         scratch_shapes=[
             pltpu.VMEM(layer_grad.shape, jnp.bfloat16),
@@ -392,19 +397,19 @@
             pltpu.VMEM((ring, 2, yc, *chunk), jnp.bfloat16),
             pltpu.VMEM((zl, yc, *chunk), jnp.bfloat16),
             pltpu.VMEM((zl, 2 * hidden, width), jnp.bfloat16),
-            pltpu.VMEM((2, 2, 2, 2 * yc * MAIN, 2 * hidden), jnp.float32),
-            pltpu.VMEM((2, 2, 2, yc * (MAIN + TAIL), hidden), jnp.bfloat16),
-            pltpu.VMEM((2, 2, 2, yc * (MAIN + TAIL), hidden), jnp.bfloat16),
+            pltpu.VMEM((2, 2, 2 * yc * MAIN, 2 * hidden), jnp.float32),
+            pltpu.VMEM((2, 2, yc * (MAIN + TAIL), hidden), jnp.bfloat16),
+            pltpu.VMEM((2, 2, yc * (MAIN + TAIL), hidden), jnp.bfloat16),
             dma((zl,)),
             dma((2, yc)), dma((2, yc)),
             dma((2, steps, 2)), dma((2, steps, 2)),
             dma((2, half + 1, 2)), dma((2, half + 1, 2)),
-            dma((ring,)), dma((ring,)),
+            dma((ring, 2)), dma((ring, 2)),
             dma((zl,)), dma((zl,)),
             dma((2, 2)), dma((2, 2)),
         ],
         compiler_params=pltpu.CompilerParams(
-            collective_id=0, has_side_effects=True, vmem_limit_bytes=62 * 1024 * 1024
+            collective_id=0, has_side_effects=True, vmem_limit_bytes=56 * 1024 * 1024
         ),
         cost_estimate=pl.CostEstimate(
             flops=2 * total * hidden * width * zl,

time: 92 us -> 90.8 us (0.987)
  the two profiles are of different devices: /device:TPU:1 before, /device:TPU:8 now
where the time goes in v3:
time: 90.8 us; the launch traced here: 90.7 us
  Pallas kernels  89.7 us (99%)
  local copies, waits for them, and re-layouts  0.95 us (1%)
    pallas_call x1, Pallas kernels, body(): pl.pallas_call(functools.partial(kernel, (dp, yc, zl, width)), out_shape=...  89.7 us

profile of v3, /device:TPU:8, one launch (start us, length us, event | category | flops | bytes accessed | tf_op | source)
XLA Modules:
  0.0 90.7 jit_solution(3601851328499880708)
XLA Ops:
  0.0 89.7 %shard_map.46 = bf16[1,1280,384]{2,1,0:T(8,128)(2,1)S(1)} custom-call(bf16[128,512]{1,0:T(8,128)(2,1)} %feats_in.1, f32[2,128]{1,0:T(2,128)} %bitcast.2, s32[2,128]{1,0:T(2,128)} %bitcast.3, bf16[1,384,4096]{2,1,0:T(8,128)(2,1)} %weight.1), custom_call_target="tpu_custom_call" | custom-call | flops 4026531840 | bytes 4128768 | tf_op jit(solution)/shard_map/pallas_call | solution.py:386
  89.7 0.9 %copy.6 = bf16[1,1280,384]{2,1,0:T(8,128)(2,1)} copy(bf16[1,1280,384]{2,1,0:T(8,128)(2,1)S(1)} %shard_map.46) | data formatting | bytes 1966080

commit v4 on v3

--- a/solution.py
+++ b/solution.py
@@ -16,7 +16,7 @@
     shape,
     feats_in, probs_in, ids_in, weight, out,
     feats, probs, ids, in_sem, routed, rows, passing, weights, acc, sums_out, sums_in, w_sem,
-    a_send, a_recv, z_send, z_recv, t_send, t_recv, x_send, x_recv, v_send, v_recv, s_send, s_recv,
+    a_send, a_recv, z_send, z_recv, t_send, t_recv, x_send, x_recv, v_send, v_recv, s_send, s_recv, e_send, e_recv,
 ):
     dp, yc, zl, width = shape
     half = zl // 2
@@ -196,15 +196,57 @@
         def _():
             t_copy(way, step, h, True).start()
 
-    def x_copy(unit, h):
-        return pltpu.make_async_remote_copy(
-            src_ref=rows.at[unit, 0, pl.ds(h * piece, piece)],
-            dst_ref=rows.at[unit, 1, pl.ds(h * piece, piece)],
+    extra = max(yc // 4, 1)
+
+    def x_copy(unit, h, less=0):
+        return pltpu.make_async_remote_copy(
+            src_ref=rows.at[unit, 0, pl.ds(h * piece, piece - less)],
+            dst_ref=rows.at[unit, 1, pl.ds(h * piece, piece - less)],
             send_sem=x_send.at[unit, h],
             recv_sem=x_recv.at[unit, h],
             device_id=at_x(beside),
             device_id_type=MESH,
         )
+
+    hold = half
+
+    def x_start(way, step, h):
+        near = step <= along(way)
+
+        @pl.when(near)
+        def _():
+            x_copy(unit_of(way, step), h, extra * h).start()
+
+        @pl.when(~near & (step <= along(way) + half))
+        def _():
+            x_copy(unit_of(way, step), h).start()
+
+    def e_place(way, step):
+        return rows.at[unit_of(way, step), 1, pl.ds(yc - extra, extra)]
+
+    def e_copy(way, step):
+        return pltpu.make_async_remote_copy(
+            src_ref=e_place(way, step),
+            dst_ref=e_place(way, step),
+            send_sem=e_send.at[way, step],
+            recv_sem=e_recv.at[way, step + 1],
+            device_id=at_ring(p + (-1 if way else 1)),
+            device_id_type=MESH,
+        )
+
+    def e_start(way, step):
+        @pl.when((along(way) < zl - 1) & (step <= along(way)))
+        def _():
+            e_copy(way, step).start()
+
+    def release():
+        def early(step, carry):
+            for h in range(2):
+                for way in range(2):
+                    x_start(way, step, h)
+            return carry
+
+        lax.fori_loop(1, hold + 1, early, 0)
 
     def z_round(step):
         for h in range(2):
@@ -216,9 +258,9 @@
 
                 z_start(way, step, h)
 
-                @pl.when(step <= along(way) + half)
+                @pl.when(step > hold)
                 def _():
-                    x_copy(unit_of(way, step), h).start()
+                    x_start(way, step, h)
 
                 @pl.when(step <= along(way) - half)
                 def _():
@@ -231,9 +273,21 @@
 
     def work(m):
         unit = unit_at(m)
-        for h in range(2):
-            place = rows.at[unit, 1, pl.ds(h * piece, piece)]
+        near = (m < zl) & (m > 0)
+
+        def x_arrived(h, less):
+            place = rows.at[unit, 1, pl.ds(h * piece, piece - less)]
             pltpu.make_async_copy(place, place, x_recv.at[unit, h]).wait()
+
+        x_arrived(0, 0)
+
+        @pl.when(near)
+        def _():
+            x_arrived(1, extra)
+
+        @pl.when(~near & (m > 0))
+        def _():
+            x_arrived(1, 0)
         zone, s = unit // zl, unit % zl
 
         @pl.when(m < zl)
@@ -323,19 +377,40 @@
     def turn(r, carry):
         z_round(r + 1)
 
+        @pl.when(r == 0)
+        def _():
+            place = rows.at[p, 1, pl.ds(piece, piece)]
+            pltpu.make_async_copy(place, place, x_recv.at[p, 1]).wait()
+
+        for way in range(2):
+            @pl.when((r > 0) & (r <= along(way)))
+            def _():
+                place = e_place(way, r)
+                pltpu.make_async_copy(place, place, e_recv.at[way, r]).wait()
+
+            e_start(way, r)
+
+        @pl.when(r + 1 == hold)
+        def _():
+            release()
+
 
         @pl.when(r >= late)
         def _():
-            work(2 * (r - late))
-            work(2 * (r - late) + 1)
-
-        @pl.when(r == late + zl // 2 - 1)
+            for i in range(3):
+                m = 3 * (r - late) + i
+
+                @pl.when(m < ring)
+                def _():
+                    work(m)
+
+        @pl.when(r == late + (zl - 1) // 3)
         def _():
             give(zh)
 
         return carry
 
-    lax.fori_loop(0, late + zl, turn, 0)
+    lax.fori_loop(0, late + (ring + 2) // 3, turn, 0)
     give(1 - zh)
     keep(zh)
     take(zh)
@@ -363,8 +438,21 @@
                 def _():
                     t_copy(way, step, h, False).wait_send()
 
-        for h in range(2):
-            x_copy(step, h).wait_send()
+            @pl.when((q < zl - 1) & (step <= q))
+            def _():
+                e_copy(way, step).wait_send()
+
+        near = (step // zl == zh) & (step != p)
+        x_copy(step, 0).wait_send()
+
+        @pl.when(near)
+        def _():
+            x_copy(step, 1, extra).wait_send()
+
+        @pl.when(~near)
+        def _():
+            x_copy(step, 1).wait_send()
+
         return carry
 
     lax.fori_loop(0, ring, left, 0)
@@ -407,6 +495,7 @@
             dma((ring, 2)), dma((ring, 2)),
             dma((zl,)), dma((zl,)),
             dma((2, 2)), dma((2, 2)),
+            dma((2, zl + 1)), dma((2, zl + 1)),
         ],
         compiler_params=pltpu.CompilerParams(
             collective_id=0, has_side_effects=True, vmem_limit_bytes=56 * 1024 * 1024

time: 90.8 us -> 87.1 us (0.959)
  the two profiles are of different devices: /device:TPU:8 before, /device:TPU:1 now
where the time goes in v4:
time: 87.1 us; the launch traced here: 86.4 us
  Pallas kernels  85.4 us (98%)
  local copies, waits for them, and re-layouts  0.95 us (1%)
    pallas_call x1, Pallas kernels, body(): pl.pallas_call(functools.partial(kernel, (dp, yc, zl, width)), out_shape=...  85.4 us

profile of v4, /device:TPU:1, one launch (start us, length us, event | category | flops | bytes accessed | tf_op | source)
XLA Modules:
  0.0 86.4 jit_solution(9375930020604961249)
XLA Ops:
  0.0 85.4 %shard_map.46 = bf16[1,1280,384]{2,1,0:T(8,128)(2,1)S(1)} custom-call(bf16[128,512]{1,0:T(8,128)(2,1)} %feats_in.1, f32[2,128]{1,0:T(2,128)} %bitcast.2, s32[2,128]{1,0:T(2,128)} %bitcast.3, bf16[1,384,4096]{2,1,0:T(8,128)(2,1)} %weight.1), custom_call_target="tpu_custom_call" | custom-call | flops 4026531840 | bytes 4128768 | tf_op jit(solution)/shard_map/pallas_call | solution.py:474
  85.4 0.9 %copy.6 = bf16[1,1280,384]{2,1,0:T(8,128)(2,1)} copy(bf16[1,1280,384]{2,1,0:T(8,128)(2,1)S(1)} %shard_map.46) | data formatting | bytes 1966080

commit v5 on v4

--- a/solution.py
+++ b/solution.py
@@ -101,25 +101,6 @@
 
     got, scale = gather([jnp.where(ranks[k] < MAIN, who[k] * MAIN + ranks[k], -1) for k in range(2)], row)
     routed[:, :, 0:width] = (got * scale).astype(jnp.bfloat16).reshape(experts, MAIN, width)
-    pl.semaphore_wait(barrier, len(partners))
-
-    beside = jnp.where((x + c) % 2 == 0, -1, 1)
-
-    def v_copy(s):
-        return pltpu.make_async_remote_copy(
-            src_ref=weights.at[s, pl.ds(0, hidden)],
-            dst_ref=weights.at[s, pl.ds(hidden, hidden)],
-            send_sem=v_send.at[s],
-            recv_sem=v_recv.at[s],
-            device_id=at_x(-beside),
-            device_id_type=MESH,
-        )
-
-    for s in range(zl):
-        w_copies[s].wait()
-    for m in range(zl):
-        v_copy(unit_at(m) % zl).start()
-
     got, scale = gather(
         [jnp.where(ranks[k] >= MAIN, who[k] * TAIL + ranks[k] - MAIN, -1) for k in range(2)],
         row // MAIN * TAIL + row % TAIL,
@@ -129,6 +110,20 @@
         tail = tail + jnp.where(sub == q, got[:, q * quarter : (q + 1) * quarter], 0.0)
     routed[:, :, width : width + quarter] = (tail * scale).astype(jnp.bfloat16).reshape(experts, MAIN, quarter)
 
+    pl.semaphore_wait(barrier, len(partners))
+
+    beside = jnp.where((x + c) % 2 == 0, -1, 1)
+
+    def v_copy(s):
+        return pltpu.make_async_remote_copy(
+            src_ref=weights.at[s, pl.ds(0, hidden)],
+            dst_ref=weights.at[s, pl.ds(hidden, hidden)],
+            send_sem=v_send.at[s],
+            recv_sem=v_recv.at[s],
+            device_id=at_x(-beside),
+            device_id_type=MESH,
+        )
+
     def a_copy(i, other):
         target = (c + i) % yc
         source = routed.at[((1 - zh) if other else zh) * yc + target]
@@ -141,10 +136,11 @@
             device_id_type=MESH,
         )
 
-    def a_arrived(i, other):
-        origin = (c + yc - i) % yc
-        place = passing.at[j, origin] if other else rows.at[p, 0, origin]
-        pltpu.make_async_copy(place, place, a_recv.at[other, i]).wait()
+    def a_arrived(origin, other):
+        @pl.when(origin != c)
+        def _():
+            place = passing.at[j, origin] if other else rows.at[p, 0, origin]
+            pltpu.make_async_copy(place, place, a_recv.at[other, (c - origin + yc) % yc]).wait()
 
     piece = yc // 2
 
@@ -353,22 +349,27 @@
             pltpu.make_async_copy(place, place, s_recv.at[zone, col]).wait()
             store(x + (2 if col else -beside), zone, sums_in[zone, col])
 
-    for other in range(2):
-        for i in range(1, yc):
-            a_copy(i, other).start()
+    for i in range(1, yc):
+        a_copy(i, 0).start()
+    for s in range(zl):
+        w_copies[s].wait()
+    for m in range(zl):
+        v_copy(unit_at(m) % zl).start()
+    for i in range(1, yc):
+        a_copy(i, 1).start()
     rows[p, 0, c] = routed[zh * yc + c]
     passing[j, c] = routed[(1 - zh) * yc + c]
     acc[...] = jnp.zeros_like(acc)
-    for i in range(1, yc):
-        a_arrived(i, 0)
     for h in range(2):
+        for origin in range(h * piece, (h + 1) * piece):
+            a_arrived(origin, 0)
         for way in range(2):
             z_start(way, 0, h)
     for h in range(2):
         x_copy(p, h).start()
-    for i in range(1, yc):
-        a_arrived(i, 1)
     for h in range(2):
+        for origin in range(h * piece, (h + 1) * piece):
+            a_arrived(origin, 1)
         for way in range(2):
             t_start(way, 0, h)
 

time: 87.1 us -> 86.8 us (level)
  no operation moved by 1% of the time
where the time goes in v5:
time: 86.8 us; the launch traced here: 86.7 us
  Pallas kernels  85.8 us (99%)
  local copies, waits for them, and re-layouts  0.95 us (1%)
    pallas_call x1, Pallas kernels, body(): pl.pallas_call(functools.partial(kernel, (dp, yc, zl, width)), out_shape=...  85.8 us

profile of v5, /device:TPU:1, one launch (start us, length us, event | category | flops | bytes accessed | tf_op | source)
XLA Modules:
  0.0 86.7 jit_solution(17741551083256566933)
XLA Ops:
  0.0 85.8 %shard_map.46 = bf16[1,1280,384]{2,1,0:T(8,128)(2,1)S(1)} custom-call(bf16[128,512]{1,0:T(8,128)(2,1)} %feats_in.1, f32[2,128]{1,0:T(2,128)} %bitcast.2, s32[2,128]{1,0:T(2,128)} %bitcast.3, bf16[1,384,4096]{2,1,0:T(8,128)(2,1)} %weight.1), custom_call_target="tpu_custom_call" | custom-call | flops 4026531840 | bytes 4128768 | tf_op jit(solution)/shard_map/pallas_call | solution.py:475
  85.8 0.9 %copy.6 = bf16[1,1280,384]{2,1,0:T(8,128)(2,1)} copy(bf16[1,1280,384]{2,1,0:T(8,128)(2,1)S(1)} %shard_map.46) | data formatting | bytes 1966080

commit v6 on v5

--- a/solution.py
+++ b/solution.py
@@ -267,6 +267,20 @@
 
     count = yc * MAIN
 
+    def multiply(unit, first, number):
+        zone, w = unit // zl, weights[unit % zl]
+        contract = (((1,), (1,)), ((), ()))
+        total = number * count
+        at = pl.ds(first * count, total)
+        whole = rows[unit, first : first + number, :, :, 0:width].reshape(total, width)
+        acc[zone, 0, at] += lax.dot_general(whole, w, contract, preferred_element_type=jnp.float32)
+        quarters = rows[unit, first : first + number, :, :, width : width + quarter].reshape(total, quarter)
+        of = lax.broadcasted_iota(jnp.int32, (total, quarter), 0) % MAIN // TAIL
+        spread = jnp.concatenate(
+            [jnp.where(of == q, quarters, jnp.zeros_like(quarters)) for q in range(4)], axis=1
+        )
+        acc[zone, 1, at] += lax.dot_general(spread, w, contract, preferred_element_type=jnp.float32)
+
     def work(m):
         unit = unit_at(m)
         near = (m < zl) & (m > 0)
@@ -284,23 +298,14 @@
         @pl.when(~near & (m > 0))
         def _():
             x_arrived(1, 0)
-        zone, s = unit // zl, unit % zl
+        s = unit % zl
 
         @pl.when(m < zl)
         def _():
             theirs = weights.at[s, pl.ds(hidden, hidden)]
             pltpu.make_async_copy(theirs, theirs, v_recv.at[s]).wait()
 
-        w = weights[s]
-        contract = (((1,), (1,)), ((), ()))
-        whole = rows[unit, :, :, :, 0:width].reshape(2 * count, width)
-        acc[zone, 0] += lax.dot_general(whole, w, contract, preferred_element_type=jnp.float32)
-        quarters = rows[unit, :, :, :, width : width + quarter].reshape(2 * count, quarter)
-        of = lax.broadcasted_iota(jnp.int32, (2 * count, quarter), 0) % MAIN // TAIL
-        spread = jnp.concatenate(
-            [jnp.where(of == q, quarters, jnp.zeros_like(quarters)) for q in range(4)], axis=1
-        )
-        acc[zone, 1] += lax.dot_general(spread, w, contract, preferred_element_type=jnp.float32)
+        multiply(unit, 0, 2)
 
     slots = MAIN + TAIL
     out_row = lax.broadcasted_iota(jnp.int32, (yc * slots, yc * (MAIN + 8)), 0)
@@ -330,10 +335,9 @@
         at = pl.ds(col * count, count)
         return in_order(acc[zone, 0, at, cols], acc[zone, 1, at, cols]).astype(jnp.bfloat16)
 
-    def give(zone):
-        for col in range(2):
-            sums_out[zone, col] = part(zone, col, pl.ds(hidden, hidden))
-            s_copy(zone, col).start()
+    def give(zone, col):
+        sums_out[zone, col] = part(zone, col, pl.ds(hidden, hidden))
+        s_copy(zone, col).start()
 
     def store(column, zone, value):
         start = pl.multiple_of(((column + dp) % dp * 2 + zone) * yc * slots, MAIN)
@@ -401,18 +405,29 @@
             for i in range(3):
                 m = 3 * (r - late) + i
 
-                @pl.when(m < ring)
+                @pl.when(m < ring - 2)
                 def _():
                     work(m)
 
         @pl.when(r == late + (zl - 1) // 3)
         def _():
-            give(zh)
+            for col in range(2):
+                give(zh, col)
 
         return carry
 
     lax.fori_loop(0, late + (ring + 2) // 3, turn, 0)
-    give(1 - zh)
+
+    last = [unit_at(ring - 2), unit_at(ring - 1)]
+    for unit in last:
+        multiply(unit, 0, 1)
+    give(1 - zh, 0)
+    for unit in last:
+        for h in range(2):
+            place = rows.at[unit, 1, pl.ds(h * piece, piece)]
+            pltpu.make_async_copy(place, place, x_recv.at[unit, h]).wait()
+        multiply(unit, 1, 1)
+    give(1 - zh, 1)
     keep(zh)
     take(zh)
     keep(1 - zh)

time: 86.8 us -> 86 us (level)
  Pallas kernels: 85.8 us -> 84.5 us
    pallas_call x1, Pallas kernels: 85.8 us -> 84.5 us  [body(): pl.pallas_call(functools.partial(kernel, (dp, yc, zl, width)), out_shape=...]
where the time goes in v6:
time: 86 us; the launch traced here: 85.4 us
  Pallas kernels  84.5 us (98%)
  local copies, waits for them, and re-layouts  0.95 us (1%)
    pallas_call x1, Pallas kernels, body(): pl.pallas_call(functools.partial(kernel, (dp, yc, zl, width)), out_shape=...  84.5 us

profile of v6, /device:TPU:1, one launch (start us, length us, event | category | flops | bytes accessed | tf_op | source)
XLA Modules:
  0.0 85.4 jit_solution(8127984385599164267)
XLA Ops:
  0.0 84.5 %shard_map.46 = bf16[1,1280,384]{2,1,0:T(8,128)(2,1)S(1)} custom-call(bf16[128,512]{1,0:T(8,128)(2,1)} %feats_in.1, f32[2,128]{1,0:T(2,128)} %bitcast.2, s32[2,128]{1,0:T(2,128)} %bitcast.3, bf16[1,384,4096]{2,1,0:T(8,128)(2,1)} %weight.1), custom_call_target="tpu_custom_call" | custom-call | flops 4026531840 | bytes 4128768 | tf_op jit(solution)/shard_map/pallas_call | solution.py:490
  84.5 0.9 %copy.6 = bf16[1,1280,384]{2,1,0:T(8,128)(2,1)} copy(bf16[1,1280,384]{2,1,0:T(8,128)(2,1)S(1)} %shard_map.46) | data formatting | bytes 1966080
